TPU v7x, 32 devices: a whole 2x2x4 slice. The times are simulated.
32 devices in a mesh: band: 2 (over y), lon: 4 (over z), lat: 2 (over x), lev: 2 (over core).
Axes of the slice: x: 2, y: 2, z: 4, core: 2. Of those that a mesh axis runs over, the one named last changes fastest.
Arguments:
- tracers: float32 [2, 128, 32, 512], P(None, 'lev', 'lon', ('band', 'lat')), parts along dimension 3, may hold values from -6 to 6
- winds: float32 [2, 128, 32, 512], P(None, 'lev', 'lon', ('band', 'lat')), parts along dimension 3, may hold values from -0.24 to 0.24
- surface_class: int32 [4, 32, 1], P(('band', 'lat'), 'lon'), parts along dimension 0, may hold values from 0 to 3; in each aligned block of 8 rows (0 to 7, 8 to 15, ..., all dimensions but the last counted through in order) at most 4 rows name the same one
- w_in: bfloat16 [4, 256, 1024], P('lon', None, 'lev'), may hold values from -0.375 to 0.375
- b_in: bfloat16 [4, 1024], P('lon', 'lev'), may hold values from -4 to 4
- w_out: bfloat16 [4, 1024, 256], P('lon', 'lev'), may hold values from -0.1875 to 0.1875
- b_out: bfloat16 [4, 256], P('lon', 'lev'), may hold values from -3 to 3
Outputs:
- new_state: float32 [2, 128, 32, 512], P(None, 'lev', 'lon', ('band', 'lat')), parts along dimension 3
There are 2 independent parts, one for each index of `band`. A program takes and returns all parts, laid end to end along the dimension named above; an argument that names none is the same for every part. Nothing has to cross between parts.
Inputs may be any that keep to these rules, and one draw needn't show every extreme that they name: `surface_class`: within the 8 blocks of one tile no class is named more than 4 times; some class reaches 4 in some tiles.
All inputs are finite; a program needn't handle non-finite values.
Results may differ from a plain program's by a relative error of at most 0.0095.
Values may be sent and summed in bfloat16 or wider, within the bound.
A program may use at most 64 MiB of HBM per device.

v0:
```python
import jax
import jax.numpy as jnp
from jax import lax
from jax.sharding import PartitionSpec as P

NSUB = 2


def extended(block, sides, width, periodic):
    for axis, dim in sides:
        count = lax.axis_size(axis)
        forward = [(i, i + 1) for i in range(count - 1)]
        if periodic:
            forward.append((count - 1, 0))
        backward = [(target, source) for source, target in forward]
        low = lax.ppermute(
            lax.slice_in_dim(block, block.shape[dim] - width, None, axis=dim), axis, forward
        )
        high = lax.ppermute(lax.slice_in_dim(block, 0, width, axis=dim), axis, backward)
        block = jnp.concatenate([low, block, high], axis=dim)
    return block


def advance(field, wind):
    east = 0.5 * (wind[0, :, :-1, :] + wind[0, :, 1:, :])
    flux_x = (
        jnp.maximum(east, 0.0) * field[:, :, :-1, :] + jnp.minimum(east, 0.0) * field[:, :, 1:, :]
    )
    north = 0.5 * (wind[1, :, :, :-1] + wind[1, :, :, 1:])
    flux_y = (
        jnp.maximum(north, 0.0) * field[:, :, :, :-1] + jnp.minimum(north, 0.0) * field[:, :, :, 1:]
    )
    div_x = flux_x[:, :, 1:, 1:-1] - flux_x[:, :, :-1, 1:-1]
    div_y = flux_y[:, :, 1:-1, 1:] - flux_y[:, :, 1:-1, :-1]
    return field[:, :, 1:-1, 1:-1] - div_x - div_y


def extend(field, width):
    looped = extended(field.astype(jnp.bfloat16), (("lon", 2),), width, True).astype(field.dtype)
    return extended(looped.astype(jnp.bfloat16), (("lat", 3),), width, False).astype(looped.dtype)


def network(inputs, first, bias_first, second):
    pre = jnp.einsum(
        "scf,fh->sch", inputs, first, preferred_element_type=jnp.float32
    ) + bias_first.astype(jnp.float32)
    hidden = jax.nn.silu(pre).astype(jnp.bfloat16)
    return jnp.einsum("sch,hf->scf", hidden, second, preferred_element_type=jnp.float32)


def shards(tracers, winds, surface_class, w_in, b_in, w_out, b_out):
    fields, levb, clon, clat = tracers.shape
    wind_ext = extend(winds, 1)
    state = tracers
    for step in range(NSUB):
        state = advance(extend(state, 1), wind_ext)
    columns = state.astype(jnp.bfloat16).transpose(2, 3, 0, 1).reshape(clon, clat, fields * levb)
    nlon = lax.axis_size("lon")
    cap = max(2, (2 * clon + nlon - 1) // nlon)
    slots = nlon * cap
    owners = surface_class.reshape(clon)
    positions = jnp.arange(clon, dtype=jnp.int32)
    same = owners[:, None] == owners[None, :]
    before = positions[:, None] > positions[None, :]
    rank = jnp.sum((same & before).astype(jnp.int32), axis=1)
    slot_of = owners * cap + rank
    picker = (slot_of[None, :] == jnp.arange(slots, dtype=jnp.int32)[:, None]).astype(jnp.bfloat16)
    outgoing = jnp.einsum(
        "sj,jcf->scf", picker, columns, preferred_element_type=jnp.float32
    ).astype(jnp.bfloat16)
    whole = lax.all_gather(
        lax.all_to_all(outgoing, "lon", split_axis=0, concat_axis=0, tiled=True),
        "lev",
        axis=2,
        tiled=True,
    )
    partial_value = network(whole, w_in[0], b_in[0], w_out[0])
    summed = lax.psum_scatter(
        partial_value.astype(jnp.bfloat16), "lev", scatter_dimension=2, tiled=True
    ).astype(jnp.float32)
    tendency = (summed + b_out[0].astype(jnp.float32)).astype(jnp.bfloat16)
    back = lax.all_to_all(tendency, "lon", split_axis=0, concat_axis=0, tiled=True)
    tend_blocks = jnp.einsum(
        "sj,scf->jcf", picker, back, preferred_element_type=jnp.float32
    ).astype(jnp.bfloat16)
    tendency = (
        tend_blocks.reshape(clon, clat, fields, levb).transpose(2, 3, 0, 1).astype(jnp.float32)
    )
    return state + 0.5 * tendency


def solution(mesh):
    placed = (
        P(None, "lev", "lon", ("band", "lat")),
        P(None, "lev", "lon", ("band", "lat")),
        P(("band", "lat"), "lon", None),
        P("lon", None, "lev"),
        P("lon", "lev"),
        P("lon", "lev", None),
        P("lon", "lev"),
    )
    return jax.shard_map(
        shards,
        mesh=mesh,
        in_specs=placed,
        out_specs=P(None, "lev", "lon", ("band", "lat")),
        check_vma=False,
    )
```

profile of v0, /device:TPU:0, one launch (start us, length us, event | category | flops | bytes accessed | tf_op | source)
XLA Modules:
  0.0 168.1 jit_solution(12718402865576457783)
XLA Ops:
  6.5 1.1 convert_element_type.76
  7.7 0.1 fusion.33
  7.8 5.1 %collective-permute-start.5 = (bf16[2,64,1,128]{3,2,1,0:T(2,128)(2,1)S(1)}, bf16[2,64,1,128]{3,2,1,0:T(2,128)(2,1)S(1)}, u32[]{:S(2)}, u32[]{:S(2)}) collective-permute-start(bf16[2,64,1,128]{3,2,1,0:T(2,128)(2,1)S(1)} %get-tuple-element.20), channel_id=1, source_target_pairs={{4,0},{8,4},{12,8},{0,12},{5,1},{9,5},{13,9},{1,13},{6,2},{10,6},{... | collective-permute-start | bytes 98312 | tf_op jit(solution)/shard_map/ppermute | solution.py:19
  12.9 0.1 copy.61
  13.0 3.9 %collective-permute-start.1 = (bf16[2,64,1,128]{3,1,0,2:T(8,128)(2,1)S(1)}, bf16[2,64,1,128]{3,1,0,2:T(8,128)(2,1)S(1)}, u32[]{:S(2)}, u32[]{:S(2)}) collective-permute-start(bf16[2,64,1,128]{3,1,0,2:T(8,128)(2,1)S(1)} %get-tuple-element.22), channel_id=1, source_target_pairs={{4,0},{8,4},{12,8},{0,12},{5,1},{9,5},{13,9},{1,13},{6,2},{10,6},{... | collective-permute-start | bytes 98312 | tf_op jit(solution)/shard_map/ppermute | solution.py:19
  16.9 2.1 %collective-permute-done.4 = bf16[2,64,1,128]{3,2,1,0:T(2,128)(2,1)S(1)} collective-permute-done((bf16[2,64,1,128]{3,2,1,0:T(2,128)(2,1)S(1)}, bf16[2,64,1,128]{3,2,1,0:T(2,128)(2,1)S(1)}, u32[]{:S(2)}, u32[]{:S(2)}) %collective-permute-start.4) | collective-permute-done | bytes 32800 | tf_op jit(solution)/shard_map/ppermute | solution.py:16
  19.0 0.3 pad_maximum_fusion
  19.3 0.2 fusion.29
  19.5 1.3 collective-permute-start.7
  20.8 4.6 %collective-permute-start.6 = (bf16[2,64,10,1]{3,2,1,0:T(8,128)(2,1)S(1)}, bf16[2,64,10,1]{3,2,1,0:T(8,128)(2,1)S(1)}, u32[]{:S(2)}, u32[]{:S(2)}) collective-permute-start(bf16[2,64,10,1]{3,2,1,0:T(8,128)(2,1)S(1)} %get-tuple-element.11), channel_id=1, source_target_pairs={{0,2},{1,3},{4,6},{5,7},{8,10},{9,11},{12,14},{13,15},{16,18},{17,... | collective-permute-start | bytes 7688 | tf_op jit(solution)/shard_map/ppermute | solution.py:16
  25.5 0.2 fusion.31
  25.7 1.3 collective-permute-start.3
  27.0 4.6 %collective-permute-start.2 = (bf16[2,64,10,1]{3,1,0,2:T(8,128)(2,1)S(1)}, bf16[2,64,10,1]{3,1,0,2:T(8,128)(2,1)S(1)}, u32[]{:S(2)}, u32[]{:S(2)}) collective-permute-start(bf16[2,64,10,1]{3,1,0,2:T(8,128)(2,1)S(1)} %get-tuple-element.15), channel_id=1, source_target_pairs={{0,2},{1,3},{4,6},{5,7},{8,10},{9,11},{12,14},{13,15},{16,18},{17,... | collective-permute-start | bytes 7688 | tf_op jit(solution)/shard_map/ppermute | solution.py:16
  31.6 4.7 %collective-permute-done.7 = bf16[2,64,10,1]{3,2,1,0:T(8,128)(2,1)S(1)} collective-permute-done((bf16[2,64,10,1]{3,2,1,0:T(8,128)(2,1)S(1)}, bf16[2,64,10,1]{3,2,1,0:T(8,128)(2,1)S(1)}, u32[]{:S(2)}, u32[]{:S(2)}) %collective-permute-start.7) | collective-permute-done | bytes 2592 | tf_op jit(solution)/shard_map/ppermute | solution.py:19
  36.3 1.5 collective-permute-done.6
  37.7 1.1 maximum_convert_fusion
  38.8 0.4 maximum_bitcast_fusion
  39.2 0.3 maximum_bitcast_fusion.1
  39.6 0.4 copy.44
  40.0 0.4 copy.43
  40.4 0.3 copy.42
  40.7 0.3 copy.41
  41.1 0.9 collective-permute-done.2
  42.0 0.4 maximum_convert_fusion.1
  42.4 0.5 fusion.6
  42.9 0.2 fusion.10
  43.1 0.0 copy-start.4
  43.1 0.6 fusion.16
  43.7 2.0 %collective-permute-start.9 = (bf16[2,64,1,128]{3,1,0,2:T(8,128)(2,1)S(1)}, bf16[2,64,1,128]{3,1,0,2:T(8,128)(2,1)S(1)}, u32[]{:S(2)}, u32[]{:S(2)}) collective-permute-start(bf16[2,64,1,128]{3,1,0,2:T(8,128)(2,1)S(1)} %get-tuple-element.18), channel_id=1, source_target_pairs={{4,0},{8,4},{12,8},{0,12},{5,1},{9,5},{13,9},{1,13},{6,2},{10,6},{... | collective-permute-start | bytes 98312 | tf_op jit(solution)/shard_map/ppermute | solution.py:19
  45.7 0.1 collective-permute-start.8
  45.8 0.2 convert_reduce_fusion
  46.0 2.0 %collective-permute-done.9 = bf16[2,64,1,128]{3,1,0,2:T(8,128)(2,1)S(1)} collective-permute-done((bf16[2,64,1,128]{3,1,0,2:T(8,128)(2,1)S(1)}, bf16[2,64,1,128]{3,1,0,2:T(8,128)(2,1)S(1)}, u32[]{:S(2)}, u32[]{:S(2)}) %collective-permute-start.9) | collective-permute-done | bytes 32800 | tf_op jit(solution)/shard_map/ppermute | solution.py:19
  48.0 3.5 %collective-permute-done.8 = bf16[2,64,1,128]{3,1,0,2:T(8,128)(2,1)S(1)} collective-permute-done((bf16[2,64,1,128]{3,1,0,2:T(8,128)(2,1)S(1)}, bf16[2,64,1,128]{3,1,0,2:T(8,128)(2,1)S(1)}, u32[]{:S(2)}, u32[]{:S(2)}) %collective-permute-start.8) | collective-permute-done | bytes 32800 | tf_op jit(solution)/shard_map/ppermute | solution.py:16
  51.5 0.2 fusion.30
  51.7 1.3 collective-permute-start.11
  53.0 4.6 %collective-permute-start.10 = (bf16[2,64,10,1]{3,1,0,2:T(8,128)(2,1)S(1)}, bf16[2,64,10,1]{3,1,0,2:T(8,128)(2,1)S(1)}, u32[]{:S(2)}, u32[]{:S(2)}) collective-permute-start(bf16[2,64,10,1]{3,1,0,2:T(8,128)(2,1)S(1)} %get-tuple-element.13), channel_id=1, source_target_pairs={{0,2},{1,3},{4,6},{5,7},{8,10},{9,11},{12,14},{13,15},{16,18},{17,... | collective-permute-start | bytes 7688 | tf_op jit(solution)/shard_map/ppermute | solution.py:16
  57.6 3.1 %collective-permute-done.11 = bf16[2,64,10,1]{3,1,0,2:T(8,128)(2,1)S(1)} collective-permute-done((bf16[2,64,10,1]{3,1,0,2:T(8,128)(2,1)S(1)}, bf16[2,64,10,1]{3,1,0,2:T(8,128)(2,1)S(1)}, u32[]{:S(2)}, u32[]{:S(2)}) %collective-permute-start.11) | collective-permute-done | bytes 2592 | tf_op jit(solution)/shard_map/ppermute | solution.py:19
  60.6 1.5 collective-permute-done.10
  62.1 0.4 maximum_convert_fusion.2
  62.5 0.5 fusion.5
  63.0 0.2 fusion.9
  63.2 0.6 fusion.27
  63.8 0.2 copy.45
  64.0 0.4 convolution_convert_fusion
  64.5 0.1 copy.46
  64.6 13.4 %all_to_all.10 = bf16[16,128,128]{2,1,0:T(8,128)(2,1)} all-to-all(bf16[16,128,128]{2,1,0:T(8,128)(2,1)S(1)} %copy.46), channel_id=1, replica_groups=mesh['band'=2,'lon'=4,'lat'=2,'lev'=2] {'lon'}, dimensions={0} | all-to-all | bytes 1048576 | tf_op jit(solution)/shard_map/all_to_all | solution.py:72
  78.0 0.0 all-gather.2.cloned.1.call-update
  78.0 0.2 reduce-scatter.4.cloned.1.call-start
  78.3 8.8 %all-gather.2.cloned.1.call-done = bf16[16,128,256]{2,1,0:T(8,128)(2,1)} async-done(((bf16[16,128,128]{2,1,0:T(8,128)(2,1)}), bf16[16,128,256]{2,1,0:T(8,128)(2,1)}) %all-gather.2.cloned.1.call-update) | async-done | bytes 1048592 | tf_op jit(solution)/shard_map/all_gather | solution.py:71
  87.1 2.6 %multiply_convert_fusion = bf16[16,128,512]{2,1,0:T(8,128)(2,1)S(1)} fusion(bf16[16,128,256]{2,1,0:T(8,128)(2,1)} %all-gather.2.cloned.1.call-done, f32[512]{0:T(512)S(1)} %bitcast.41, bf16[1,256,512]{2,1,0:T(8,128)(2,1)S(1)} %copy-done), kind=kOutput, calls=%fused_computation | convolution fusion | flops 543162368 | bytes 3409920 | tf_op jit(solution)/shard_map/scf,fh->sch/dot_general | solution.py:44
  89.7 1.4 fusion.2
  91.0 12.0 %copy.52 = bf16[16,128,256]{0,1,2:T(8,128)(2,1)} copy(bf16[16,128,256]{2,0,1:T(8,128)(2,1)S(1)} %fusion.2) | data formatting | bytes 2097152
  103.0 15.8 %reshape.41 = bf16[256,2048]{1,0:T(8,128)(2,1)} reshape(bf16[256,128,16]{2,1,0:T(8,128)(2,1)} %bitcast.37) | data formatting | bytes 2097152
  118.8 0.0 reduce-scatter.4.cloned.1.call-update
  118.8 9.9 %reduce-scatter.4.cloned.1.call-done = bf16[128,2048]{1,0:T(8,128)(2,1)} async-done(((bf16[256,2048]{1,0:T(8,128)(2,1)}), bf16[128,2048]{1,0:T(8,128)(2,1)}) %reduce-scatter.4.cloned.1.call-update) | async-done | bytes 524304
  128.7 5.4 %reshape.42 = bf16[128,128,16]{2,1,0:T(8,128)(2,1)} reshape(bf16[128,2048]{1,0:T(8,128)(2,1)} %reduce-scatter.4.cloned.1.call-done) | data formatting | bytes 1048576
  134.1 5.5 %copy.53 = bf16[16,128,128]{2,0,1:T(8,128)(2,1)S(1)} copy(bf16[16,128,128]{0,1,2:T(8,128)(2,1)} %bitcast.38) | data formatting | bytes 1048576
  139.6 0.1 add_convert_fusion
  139.7 0.1 copy.48
  139.9 19.6 %all_to_all.11 = bf16[16,128,128]{2,1,0:T(8,128)(2,1)S(1)} all-to-all(bf16[16,128,128]{2,1,0:T(8,128)(2,1)S(1)} %copy.48), channel_id=1, replica_groups=mesh['band'=2,'lon'=4,'lat'=2,'lev'=2] {'lon'}, dimensions={0} | all-to-all | bytes 1048576 | tf_op jit(solution)/shard_map/all_to_all | solution.py:82
  159.5 0.4 fusion.8
  159.9 0.2 copy.50
  160.1 0.1 add.68
  160.2 1.1 copy.51
  (25 shorter events, 0.2 us)
Async XLA Ops:
  6.5 80.5 %copy-start = (bf16[1,256,512]{2,1,0:T(8,128)(2,1)S(1)}, bf16[1,256,512]{2,1,0:T(8,128)(2,1)}, u32[]{:S(2)}) copy-start(bf16[1,256,512]{2,1,0:T(8,128)(2,1)} %param.10) | copy-start | bytes 786436
  6.5 6.4 %copy-start.1 = (f32[2,64,8,128]{3,2,1,0:T(8,128)S(1)}, f32[2,64,8,128]{3,2,1,0:T(8,128)}, u32[]{:S(2)}) copy-start(f32[2,64,8,128]{3,2,1,0:T(8,128)} %param.7) | copy-start | bytes 1572868
  6.5 80.5 %all-gather.2.cloned.1.call-start = ((), (), s32[]{:S(2)}) async-start(), calls=%async_computation.3 | async-start | bytes 1572864 | tf_op jit(solution)/shard_map/all_gather | solution.py:71
  7.8 9.1 %collective-permute-start.5 = (bf16[2,64,1,128]{3,2,1,0:T(2,128)(2,1)S(1)}, bf16[2,64,1,128]{3,2,1,0:T(2,128)(2,1)S(1)}, u32[]{:S(2)}, u32[]{:S(2)}) collective-permute-start(bf16[2,64,1,128]{3,2,1,0:T(2,128)(2,1)S(1)} %get-tuple-element.20), channel_id=1, source_target_pairs={{4,0},{8,4},{12,8},{0,12},{5,1},{9,5},{13,9},{1,13},{6,2},{10,6},{... | collective-permute-start | bytes 98312 | tf_op jit(solution)/shard_map/ppermute | solution.py:19
  12.9 6.1 %collective-permute-start.4 = (bf16[2,64,1,128]{3,2,1,0:T(2,128)(2,1)S(1)}, bf16[2,64,1,128]{3,2,1,0:T(2,128)(2,1)S(1)}, u32[]{:S(2)}, u32[]{:S(2)}) collective-permute-start(bf16[2,64,1,128]{3,2,1,0:T(2,128)(2,1)S(1)} %get-tuple-element.19), channel_id=1, source_target_pairs={{0,4},{4,8},{8,12},{12,0},{1,5},{5,9},{9,13},{13,1},{2,6},{6,10},{... | collective-permute-start | bytes 98312 | tf_op jit(solution)/shard_map/ppermute | solution.py:16
  13.0 12.4 %collective-permute-start.1 = (bf16[2,64,1,128]{3,1,0,2:T(8,128)(2,1)S(1)}, bf16[2,64,1,128]{3,1,0,2:T(8,128)(2,1)S(1)}, u32[]{:S(2)}, u32[]{:S(2)}) collective-permute-start(bf16[2,64,1,128]{3,1,0,2:T(8,128)(2,1)S(1)} %get-tuple-element.22), channel_id=1, source_target_pairs={{4,0},{8,4},{12,8},{0,12},{5,1},{9,5},{13,9},{1,13},{6,2},{10,6},{... | collective-permute-start | bytes 98312 | tf_op jit(solution)/shard_map/ppermute | solution.py:19
  16.9 8.5 %collective-permute-start = (bf16[2,64,1,128]{3,1,0,2:T(8,128)(2,1)S(1)}, bf16[2,64,1,128]{3,1,0,2:T(8,128)(2,1)S(1)}, u32[]{:S(2)}, u32[]{:S(2)}) collective-permute-start(bf16[2,64,1,128]{3,1,0,2:T(8,128)(2,1)S(1)} %get-tuple-element.21), channel_id=1, source_target_pairs={{0,4},{4,8},{8,12},{12,0},{1,5},{5,9},{9,13},{13,1},{2,6},{6,10},{... | collective-permute-start | bytes 98312 | tf_op jit(solution)/shard_map/ppermute | solution.py:16
  19.5 16.8 %collective-permute-start.7 = (bf16[2,64,10,1]{3,2,1,0:T(8,128)(2,1)S(1)}, bf16[2,64,10,1]{3,2,1,0:T(8,128)(2,1)S(1)}, u32[]{:S(2)}, u32[]{:S(2)}) collective-permute-start(bf16[2,64,10,1]{3,2,1,0:T(8,128)(2,1)S(1)} %get-tuple-element.12), channel_id=1, source_target_pairs={{2,0},{3,1},{6,4},{7,5},{10,8},{11,9},{14,12},{15,13},{18,16},{19,... | collective-permute-start | bytes 7688 | tf_op jit(solution)/shard_map/ppermute | solution.py:19
  20.8 16.9 %collective-permute-start.6 = (bf16[2,64,10,1]{3,2,1,0:T(8,128)(2,1)S(1)}, bf16[2,64,10,1]{3,2,1,0:T(8,128)(2,1)S(1)}, u32[]{:S(2)}, u32[]{:S(2)}) collective-permute-start(bf16[2,64,10,1]{3,2,1,0:T(8,128)(2,1)S(1)} %get-tuple-element.11), channel_id=1, source_target_pairs={{0,2},{1,3},{4,6},{5,7},{8,10},{9,11},{12,14},{13,15},{16,18},{17,... | collective-permute-start | bytes 7688 | tf_op jit(solution)/shard_map/ppermute | solution.py:16
  25.7 15.4 %collective-permute-start.3 = (bf16[2,64,10,1]{3,1,0,2:T(8,128)(2,1)S(1)}, bf16[2,64,10,1]{3,1,0,2:T(8,128)(2,1)S(1)}, u32[]{:S(2)}, u32[]{:S(2)}) collective-permute-start(bf16[2,64,10,1]{3,1,0,2:T(8,128)(2,1)S(1)} %get-tuple-element.16), channel_id=1, source_target_pairs={{2,0},{3,1},{6,4},{7,5},{10,8},{11,9},{14,12},{15,13},{18,16},{19,... | collective-permute-start | bytes 7688 | tf_op jit(solution)/shard_map/ppermute | solution.py:19
  27.0 15.0 %collective-permute-start.2 = (bf16[2,64,10,1]{3,1,0,2:T(8,128)(2,1)S(1)}, bf16[2,64,10,1]{3,1,0,2:T(8,128)(2,1)S(1)}, u32[]{:S(2)}, u32[]{:S(2)}) collective-permute-start(bf16[2,64,10,1]{3,1,0,2:T(8,128)(2,1)S(1)} %get-tuple-element.15), channel_id=1, source_target_pairs={{0,2},{1,3},{4,6},{5,7},{8,10},{9,11},{12,14},{13,15},{16,18},{17,... | collective-permute-start | bytes 7688 | tf_op jit(solution)/shard_map/ppermute | solution.py:16
  43.1 2.7 %copy-start.4 = (s32[1,8,1]{1,2,0:T(1,128)S(1)}, s32[1,8,1]{1,2,0:T(1,128)}, u32[]{:S(2)}) copy-start(s32[1,8,1]{1,2,0:T(1,128)} %param.9) | copy-start | bytes 100
  43.7 4.2 %collective-permute-start.9 = (bf16[2,64,1,128]{3,1,0,2:T(8,128)(2,1)S(1)}, bf16[2,64,1,128]{3,1,0,2:T(8,128)(2,1)S(1)}, u32[]{:S(2)}, u32[]{:S(2)}) collective-permute-start(bf16[2,64,1,128]{3,1,0,2:T(8,128)(2,1)S(1)} %get-tuple-element.18), channel_id=1, source_target_pairs={{4,0},{8,4},{12,8},{0,12},{5,1},{9,5},{13,9},{1,13},{6,2},{10,6},{... | collective-permute-start | bytes 98312 | tf_op jit(solution)/shard_map/ppermute | solution.py:19
  45.7 5.7 %collective-permute-start.8 = (bf16[2,64,1,128]{3,1,0,2:T(8,128)(2,1)S(1)}, bf16[2,64,1,128]{3,1,0,2:T(8,128)(2,1)S(1)}, u32[]{:S(2)}, u32[]{:S(2)}) collective-permute-start(bf16[2,64,1,128]{3,1,0,2:T(8,128)(2,1)S(1)} %get-tuple-element.17), channel_id=1, source_target_pairs={{0,4},{4,8},{8,12},{12,0},{1,5},{5,9},{9,13},{13,1},{2,6},{6,10},{... | collective-permute-start | bytes 98312 | tf_op jit(solution)/shard_map/ppermute | solution.py:16
  51.7 9.0 %collective-permute-start.11 = (bf16[2,64,10,1]{3,1,0,2:T(8,128)(2,1)S(1)}, bf16[2,64,10,1]{3,1,0,2:T(8,128)(2,1)S(1)}, u32[]{:S(2)}, u32[]{:S(2)}) collective-permute-start(bf16[2,64,10,1]{3,1,0,2:T(8,128)(2,1)S(1)} %get-tuple-element.14), channel_id=1, source_target_pairs={{2,0},{3,1},{6,4},{7,5},{10,8},{11,9},{14,12},{15,13},{18,16},{19,... | collective-permute-start | bytes 7688 | tf_op jit(solution)/shard_map/ppermute | solution.py:19
  53.0 9.1 %collective-permute-start.10 = (bf16[2,64,10,1]{3,1,0,2:T(8,128)(2,1)S(1)}, bf16[2,64,10,1]{3,1,0,2:T(8,128)(2,1)S(1)}, u32[]{:S(2)}, u32[]{:S(2)}) collective-permute-start(bf16[2,64,10,1]{3,1,0,2:T(8,128)(2,1)S(1)} %get-tuple-element.13), channel_id=1, source_target_pairs={{0,2},{1,3},{4,6},{5,7},{8,10},{9,11},{12,14},{13,15},{16,18},{17,... | collective-permute-start | bytes 7688 | tf_op jit(solution)/shard_map/ppermute | solution.py:16
  64.5 13.8 %copy-start.2 = (bf16[1,512]{1,0:T(2,128)(2,1)S(1)}, bf16[1,512]{1,0:T(2,128)(2,1)}, u32[]{:S(2)}) copy-start(bf16[1,512]{1,0:T(2,128)(2,1)} %param.11) | copy-start | bytes 3076
  78.0 50.7 %reduce-scatter.4.cloned.1.call-start = ((), (), s32[]{:S(2)}) async-start(), calls=%async_computation.4 | async-start | bytes 1572864
  87.1 2.6 %copy-start.3 = (bf16[1,512,256]{2,1,0:T(8,128)(2,1)S(1)}, bf16[1,512,256]{2,1,0:T(8,128)(2,1)}, u32[]{:S(2)}) copy-start(bf16[1,512,256]{2,1,0:T(8,128)(2,1)} %param.12) | copy-start | bytes 786436
  103.0 15.8 %copy-start.5 = (bf16[1,128]{1,0:T(2,128)(2,1)S(1)}, bf16[1,128]{1,0:T(2,128)(2,1)}, u32[]{:S(2)}) copy-start(bf16[1,128]{1,0:T(2,128)(2,1)} %param.13) | copy-start | bytes 772
Sparse Core Ops, SparseCore 0:
  78.2 8.8 all-gather.1
  118.9 9.7 reduce-scatter.3
where the time goes:
time: 169 us; the launch traced here: 168 us
  local copies, waits for them, and re-layouts  42.7 us (25%)
  waiting for transfers between devices  37.8 us (22%)
  blocking collectives  33 us (20%)
  starting transfers between devices  28.9 us (17%)
  between operations  13.8 us (8%)
  other arithmetic  7.12 us (4%)
  matrix products  4.76 us (3%)
    unnamed x17, local copies, waits for them, and re-layouts  38.8 us
    all_to_all x1, blocking collectives, shards(): lax.all_to_all(tendency, 'lon', split_axis=0, concat_axis=0, tiled=True)  19.6 us
    ppermute x6, starting transfers between devices, extended(): lax.ppermute(lax.slice_in_dim(block, 0, width, axis=dim), axis, backward)  14.9 us
    ppermute x6, starting transfers between devices, extended(): lax.ppermute(lax.slice_in_dim(block, block.shape[dim] - width, None, axis...  13.8 us
    all_to_all x1, blocking collectives, shards(): lax.all_to_all(outgoing, 'lon', split_axis=0, concat_axis=0, tiled=True)  13.4 us
    unnamed x3, waiting for transfers between devices  9.9 us
    ppermute x6, waiting for transfers between devices, extended(): lax.ppermute(lax.slice_in_dim(block, 0, width, axis=dim), axis, backward)  9.75 us
    ppermute x6, waiting for transfers between devices, extended(): lax.ppermute(lax.slice_in_dim(block, block.shape[dim] - width, None, axis...  9.41 us
  transfers between devices with their start and end apart: 14, of which 10 were waited for; matrix products, arithmetic and copies ran while one was open for 3% of the time, Pallas kernels for 0%

commit v1 on v0

v1 whole, which is shorter than its diff:
```python
import functools

import jax
import jax.numpy as jnp
from jax import lax
from jax.experimental import pallas as pl
from jax.experimental.pallas import tpu as pltpu
from jax.sharding import PartitionSpec as P

MESH = pl.DeviceIdType.MESH
F32 = jnp.float32
BF16 = jnp.bfloat16


def step(q, west, east, south, north, u_w, u, u_e, v_s, v, v_n):
    levels = u.shape[0]
    face_e = 0.5 * (u + u_e)
    face_w = 0.5 * (u_w + u)
    face_n = 0.5 * (v + v_n)
    face_s = 0.5 * (v_s + v)
    e_pos, e_neg = jnp.maximum(face_e, 0.0), jnp.minimum(face_e, 0.0)
    w_pos, w_neg = jnp.maximum(face_w, 0.0), jnp.minimum(face_w, 0.0)
    n_pos, n_neg = jnp.maximum(face_n, 0.0), jnp.minimum(face_n, 0.0)
    s_pos, s_neg = jnp.maximum(face_s, 0.0), jnp.minimum(face_s, 0.0)
    parts = []
    for f in range(q.shape[0] // levels):
        cut = slice(f * levels, (f + 1) * levels)
        c = q[cut]
        div_x = (e_pos * c + e_neg * east[cut]) - (w_pos * west[cut] + w_neg * c)
        div_y = (n_pos * c + n_neg * north[cut]) - (s_pos * south[cut] + s_neg * c)
        parts.append((c - div_x) - div_y)
    return jnp.concatenate(parts, axis=0)


def kernel(
    sizes,
    tr_ref, wd_ref, sc_ref, wi_ref, bi_ref, wo_ref, bo_ref,
    out_ref,
    hs, hr, pack, rp, tt, q1, h1, st, xbuf, pbuf, rbuf, wi_all, wo_all, bias,
    hs_sem, hr_sem, ps_sem, pr_sem, loc_sem, a_send, a_recv, b_send, b_recv,
    xs_sem, xr_sem, ys_sem, yr_sem,
):
    nband, nlon, nlat = sizes
    b, z, a, l = (lax.axis_index(n) for n in ("band", "lon", "lat", "lev"))
    clon = out_ref.shape[0] // 128
    rows_i = wi_ref.shape[1] // (nband * 2)
    rows_o = wo_ref.shape[1] // (nband * 2)
    p = b * 2 + lax.rem(a, 2)
    pair = a - lax.rem(a, 2)
    has_low, has_high = a > 0, a < nlat - 1

    def lon_at(d):
        return lax.rem(z + d + nlon, nlon)

    def peer_of(k):
        other = lax.rem(p + k, nband * 2)
        return {"band": other // 2, "lat": pair + lax.rem(other, 2)}, other

    barrier = pltpu.get_barrier_semaphore()
    for d in range(1, nlon):
        pl.semaphore_signal(barrier, inc=1, device_id={"lon": lon_at(d)}, device_id_type=MESH)
    for k in range(1, nband * 2):
        pl.semaphore_signal(barrier, inc=1, device_id=peer_of(k)[0], device_id_type=MESH)
    pl.semaphore_signal(barrier, inc=1, device_id={"lev": 1 - l}, device_id_type=MESH)
    for has, da in ((has_low, -1), (has_high, 1)):
        @pl.when(has)
        def _(da=da):
            for d in (-1, 0, 1):
                pl.semaphore_signal(
                    barrier, inc=1, device_id={"lat": a + da, "lon": lon_at(d)}, device_id_type=MESH
                )

    def own(ref, j):
        return ref[pl.ds(j, 128, stride=clon), :]

    for slot, j in enumerate((0, 1, clon - 2, clon - 1)):
        hs[slot, 0] = own(tr_ref, j).astype(BF16)
        hs[slot, 1] = own(wd_ref, j).astype(BF16)
    bias[z, :, : bi_ref.shape[1]] = jnp.broadcast_to(
        bi_ref[...].astype(F32), (16, bi_ref.shape[1])
    ).astype(BF16)
    bias[z, :, bi_ref.shape[1]:] = jnp.broadcast_to(
        bo_ref[...].astype(F32), (16, bo_ref.shape[1])
    ).astype(BF16)

    sides = (a + nlat - 1) // nlat + (2 * nlat - 2 - a) // nlat
    pl.semaphore_wait(barrier, nlon - 1 + nband * 2 - 1 + 1 + 3 * sides)

    halos = []
    for side, d in ((0, 1), (1, -1)):
        first = 2 if d == 1 else 0
        halos.append(pltpu.make_async_remote_copy(
            src_ref=hs.at[pl.ds(first, 2)], dst_ref=hr.at[side],
            send_sem=hs_sem.at[side], recv_sem=hr_sem.at[side],
            device_id={"lon": lon_at(d)}, device_id_type=MESH,
        ))
        halos[-1].start()

    lane = lax.broadcasted_iota(jnp.int32, (128, 128), 1)
    acc = jnp.zeros((128, 128), F32)
    for base, ref in ((0, tr_ref), (32, wd_ref)):
        for j in range(clon):
            x = own(ref, j)
            for g, col in enumerate((0, 1, 126, 127)):
                place = base + g * 8 + j
                acc = jnp.where(lane == place, pltpu.roll(x, (place - col) % 128, 1), acc)
    pack[...] = acc.astype(BF16)

    def pack_copy(side, d):
        return pltpu.make_async_remote_copy(
            src_ref=pack, dst_ref=rp.at[side, 1 - d],
            send_sem=ps_sem.at[side, 1 - d], recv_sem=pr_sem.at[side, 1 - d],
            device_id={"lat": a + (1 if side == 0 else -1), "lon": lon_at(d)}, device_id_type=MESH,
        )

    for has, side in ((has_low, 1), (has_high, 0)):
        @pl.when(has)
        def _(side=side):
            for d in (0, 1, -1):
                pack_copy(side, d).start()

    local = [
        pltpu.make_async_copy(wi_ref.at[0], wi_all.at[z], loc_sem.at[0]),
        pltpu.make_async_copy(wo_ref.at[0], wo_all.at[z], loc_sem.at[1]),
    ]
    cut_i, cut_o = pl.ds(p * rows_i, rows_i), pl.ds(p * rows_o, rows_o)
    firsts = []
    for d in range(1, nlon):
        trio = []
        for kind, (src, dst) in enumerate((
            (wi_ref.at[0, cut_i], wi_all.at[z, cut_i]),
            (wo_ref.at[0, cut_o], wo_all.at[z, cut_o]),
            (bias.at[z], bias.at[z]),
        )):
            trio.append(pltpu.make_async_remote_copy(
                src_ref=src, dst_ref=dst,
                send_sem=a_send.at[kind, d], recv_sem=a_recv.at[kind, d],
                device_id={"lon": lon_at(d)}, device_id_type=MESH,
            ))
            trio[-1].start()
        firsts.append(trio)
    for copy in local:
        copy.start()

    seconds = []

    def forward(d):
        for copy in firsts[d - 1]:
            copy.wait_recv()
        c = lon_at(-d)
        for k in range(1, nband * 2):
            for kind, (buf, cut) in enumerate(((wi_all, cut_i), (wo_all, cut_o))):
                copy = pltpu.make_async_remote_copy(
                    src_ref=buf.at[c, cut], dst_ref=buf.at[c, cut],
                    send_sem=b_send.at[kind, d, k], recv_sem=b_recv.at[kind, d, k],
                    device_id=peer_of(k)[0], device_id_type=MESH,
                )
                copy.start()
                seconds.append(copy)

    for has, side in ((has_low, 0), (has_high, 1)):
        @pl.when(has)
        def _(side=side):
            for d in (-1, 0, 1):
                pltpu.make_async_copy(
                    rp.at[side, 1 + d], rp.at[side, 1 + d], pr_sem.at[side, 1 + d]
                ).wait()

        @pl.when(jnp.logical_not(has))
        def _(side=side):
            rp[side] = jnp.zeros(rp.shape[1:], BF16)

    from_low = lax.rem(lane, 32) >= 16
    for d in range(3):
        tt[d] = jnp.where(from_low, rp[0, d].astype(F32), rp[1, d].astype(F32))

    first, last = lax.rem(lane, 8) == 0, lax.rem(lane, 8) == 7
    near = lax.rem(lane, 32) < 8
    mid = tt[1]
    edge = {
        "c": mid,
        "w": jnp.where(first, pltpu.roll(tt[0], 121, 1), pltpu.roll(mid, 1, 1)),
        "e": jnp.where(last, pltpu.roll(tt[2], 7, 1), pltpu.roll(mid, 127, 1)),
        "s": jnp.where(near, pltpu.roll(acc, 104, 1), pltpu.roll(mid, 8, 1)),
        "n": jnp.where(near, pltpu.roll(mid, 120, 1), pltpu.roll(acc, 24, 1)),
    }
    wind = {key: pltpu.roll(value, 96, 1) for key, value in edge.items()}
    outer = step(
        edge["c"], edge["w"], edge["e"], edge["s"], edge["n"],
        wind["w"][:64], wind["c"][:64], wind["e"][:64],
        wind["s"][64:], wind["c"][64:], wind["n"][64:],
    )
    outside = jnp.where(lane >= 16, a, nlat - 1 - a) > 0
    h1[...] = jnp.where(outside, outer, 0.0)

    def shifted(x, rim, low_lane, high_lane):
        ln = lane[: x.shape[0]]
        south = jnp.where(ln == 0, pltpu.roll(rim, (128 - low_lane) % 128, 1), pltpu.roll(x, 1, 1))
        north = jnp.where(
            ln == 127, pltpu.roll(rim, (127 - high_lane) % 128, 1), pltpu.roll(x, 127, 1)
        )
        return south, north

    def field(r):
        if r < 0:
            return hr[0, 2 + r, 0].astype(F32)
        if r >= clon:
            return hr[1, r - clon, 0].astype(F32)
        return own(tr_ref, r)

    def zonal(r):
        if r < 0:
            return hr[0, 2 + r, 1, :64].astype(F32)
        if r >= clon:
            return hr[1, r - clon, 1, :64].astype(F32)
        return wd_ref[pl.ds(r, 64, stride=clon), :]

    def merid(r):
        if r < 0:
            return hr[0, 2 + r, 1, 64:].astype(F32)
        if r >= clon:
            return hr[1, r - clon, 1, 64:].astype(F32)
        return wd_ref[pl.ds(64 * clon + r, 64, stride=clon), :]

    def rim_of(r):
        return (0, clon - 1) if r < 0 else (2, 0) if r >= clon else (1, r)

    def advance(r, get, rim):
        slot, j = rim_of(r)
        v = merid(r)
        v_s, v_n = shifted(v, tt[slot, 64:, :], 56 + j, 32 + j)
        q = get(r)
        south, north = shifted(q, rim, 24 + j, j)
        return step(
            q, get(r - 1), get(r + 1), south, north,
            zonal(r - 1), zonal(r), zonal(r + 1), v_s, v, v_n,
        )

    inner = list(range(1, clon - 1))
    for r in inner:
        q1[r + 1] = advance(r, field, tt[1])
    for copy in halos:
        copy.wait_recv()
    for r in (-1, 0, clon - 1, clon):
        q1[r + 1] = advance(r, field, tt[rim_of(r)[0]])

    def x_copy(j):
        return pltpu.make_async_remote_copy(
            src_ref=xbuf.at[l, j], dst_ref=xbuf.at[l, j],
            send_sem=xs_sem.at[j], recv_sem=xr_sem.at[j],
            device_id={"lev": 1 - l}, device_id_type=MESH,
        )

    for r in range(clon):
        new = advance(r, lambda k: q1[k + 1], h1[...])
        st[r] = new
        xbuf[l, r] = new.T.astype(BF16)
        x_copy(r).start()

    for d in range(1, nlon):
        forward(d)
    for copy in seconds:
        copy.wait_recv()
    for copy in local:
        copy.wait()

    def y_copy(j):
        return pltpu.make_async_remote_copy(
            src_ref=pbuf.at[j, 1 - l], dst_ref=rbuf.at[j],
            send_sem=ys_sem.at[j], recv_sem=yr_sem.at[j],
            device_id={"lev": 1 - l}, device_id_type=MESH,
        )

    hid = bi_ref.shape[1]

    @pl.loop(0, clon)
    def _(j):
        x_copy(j).wait_recv()
        c = sc_ref[0, j]
        x = jnp.concatenate([xbuf[0, j], xbuf[1, j]], axis=1)
        pre = jnp.dot(x, wi_all[c], preferred_element_type=F32) + bias[c][0:1, :hid].astype(F32)
        hidden = (pre * jax.nn.sigmoid(pre)).astype(BF16)
        part = jnp.dot(hidden, wo_all[c], preferred_element_type=F32).astype(BF16)
        pbuf[j, 0] = part[:, :128]
        pbuf[j, 1] = part[:, 128:]
        y_copy(j).start()

    @pl.loop(0, clon)
    def _(j):
        y_copy(j).wait_recv()
        c = sc_ref[0, j]
        total = pbuf[j, l].astype(F32) + rbuf[j].astype(F32)
        tend = (total + bias[c][0:1, hid:].astype(F32)).astype(BF16).astype(F32)
        out_ref[pl.ds(j, 128, stride=clon), :] = st[j] + 0.5 * tend.T

    for copy in halos:
        copy.wait_send()
    for has, side in ((has_low, 1), (has_high, 0)):
        @pl.when(has)
        def _(side=side):
            for d in (0, 1, -1):
                pack_copy(side, d).wait_send()
    for trio in firsts:
        for copy in trio:
            copy.wait_send()
    for copy in seconds:
        copy.wait_send()

    @pl.loop(0, clon)
    def _(j):
        x_copy(j).wait_send()
        y_copy(j).wait_send()


def shards(sizes, tracers, winds, surface_class, w_in, b_in, w_out, b_out):
    fields, levb, clon, clat = tracers.shape
    nband, nlon, nlat = sizes
    rows = fields * levb
    flat = (rows * clon, clat)
    members = nband * 2
    vmem = pl.BlockSpec(memory_space=pltpu.VMEM)
    smem = pl.BlockSpec(memory_space=pltpu.SMEM)
    anywhere = pl.BlockSpec(memory_space=pl.ANY)
    dma = pltpu.SemaphoreType.DMA
    new = pl.pallas_call(
        functools.partial(kernel, sizes),
        out_shape=jax.ShapeDtypeStruct(flat, F32),
        in_specs=[vmem, vmem, smem, anywhere, vmem, anywhere, vmem],
        out_specs=vmem,
        scratch_shapes=[
            pltpu.VMEM((4, 2, rows, clat), BF16),
            pltpu.VMEM((2, 2, 2, rows, clat), BF16),
            pltpu.VMEM((rows, clat), BF16),
            pltpu.VMEM((2, 3, rows, clat), BF16),
            pltpu.VMEM((3, rows, clat), F32),
            pltpu.VMEM((clon + 2, rows, clat), F32),
            pltpu.VMEM((rows, clat), F32),
            pltpu.VMEM((clon, rows, clat), F32),
            pltpu.VMEM((2, clon, clat, rows), BF16),
            pltpu.VMEM((clon, 2, clat, rows), BF16),
            pltpu.VMEM((clon, clat, rows), BF16),
            pltpu.VMEM((nlon,) + w_in.shape[1:], BF16),
            pltpu.VMEM((nlon,) + w_out.shape[1:], BF16),
            pltpu.VMEM((nlon, 16, b_in.shape[1] + b_out.shape[1]), BF16),
            dma((2,)), dma((2,)), dma((2, 3)), dma((2, 3)), dma((2,)),
            dma((3, nlon)), dma((3, nlon)), dma((2, nlon, members)), dma((2, nlon, members)),
            dma((clon,)), dma((clon,)), dma((clon,)), dma((clon,)),
        ],
        compiler_params=pltpu.CompilerParams(
            collective_id=0, has_side_effects=True, vmem_limit_bytes=48 * 1024 * 1024
        ),
    )(tracers.reshape(flat), winds.reshape(flat), surface_class.reshape(1, clon), w_in, b_in, w_out, b_out)
    return new.reshape(tracers.shape)


def solution(mesh):
    placed = (
        P(None, "lev", "lon", ("band", "lat")),
        P(None, "lev", "lon", ("band", "lat")),
        P(("band", "lat"), "lon", None),
        P("lon", None, "lev"),
        P("lon", "lev"),
        P("lon", "lev", None),
        P("lon", "lev"),
    )
    sizes = tuple(mesh.shape[name] for name in ("band", "lon", "lat"))
    return jax.shard_map(
        functools.partial(shards, sizes),
        mesh=mesh,
        in_specs=placed,
        out_specs=P(None, "lev", "lon", ("band", "lat")),
        check_vma=False,
    )
```

time: 169 us -> 49 us (0.29)
  Pallas kernels: 0 us -> 43.2 us
  waiting for transfers between devices: 37.8 us -> 0 us
  local copies, waits for them, and re-layouts: 42.7 us -> 5.46 us
  blocking collectives: 33 us -> 0 us
  starting transfers between devices: 28.9 us -> 0 us
  between operations: 13.8 us -> 0.02 us
  other arithmetic: 7.12 us -> 0 us
  matrix products: 4.76 us -> 0 us
    pallas_call x0 -> x1, Pallas kernels: none -> 43.2 us  [shards(): pl.pallas_call(functools.partial(kernel, sizes), out_shape=jax.ShapeDtype...]
    unnamed x17 -> x15, local copies, waits for them, and re-layouts: 38.8 us -> 5.46 us
    all_to_all x2 -> x0, blocking collectives: 33 us -> none  [the longest x1 19.6 us: shards(): lax.all_to_all(tendency, 'lon', split_axis=0, concat_axis=0, tiled=True)]
    ppermute x12 -> x0, starting transfers between devices: 28.7 us -> none  [the longest x6 14.9 us: extended(): lax.ppermute(lax.slice_in_dim(block, 0, width, axis=dim), axis, backward)]
    ppermute x12 -> x0, waiting for transfers between devices: 19.2 us -> none  [the longest x6 9.75 us: extended(): lax.ppermute(lax.slice_in_dim(block, 0, width, axis=dim), axis, backward)]
    unnamed x3 -> x0, waiting for transfers between devices: 9.9 us -> none
    all_gather x1 -> x0, waiting for transfers between devices: 8.78 us -> none  [shards(): lax.all_gather(lax.all_to_all(outgoing, 'lon', split_axis=0, concat_axis=...]
    dot_general x4 -> x0, matrix products: 4.76 us -> none  [the longest x1 2.58 us: network(): jnp.einsum('scf,fh->sch', inputs, first, preferred_element_type=jnp.float32)]
  transfers between devices with their start and end apart: 14 -> 0, of which waited for: 10 -> 0; matrix products, arithmetic and copies ran while one was open for 3% -> 0% of each run, Pallas kernels for 0% -> 0%
where the time goes in v1:
time: 49 us; the launch traced here: 48.7 us
  Pallas kernels  43.2 us (88%)
  local copies, waits for them, and re-layouts  5.46 us (11%)
    pallas_call x1, Pallas kernels, shards(): pl.pallas_call(functools.partial(kernel, sizes), out_shape=jax.ShapeDtype...  43.2 us
    unnamed x15, local copies, waits for them, and re-layouts  5.46 us

profile of v1, /device:TPU:0, one launch (start us, length us, event | category | flops | bytes accessed | tf_op | source)
XLA Modules:
  0.0 48.7 jit_solution(7826043295857988768)
XLA Ops:
  0.0 0.0 copy-start.4
  0.0 0.0 copy-start.5
  0.0 0.0 copy-start.6
  0.0 0.7 %copy-done.4 = bf16[1,512]{1,0:T(2,128)(2,1)S(1)} copy-done((bf16[1,512]{1,0:T(2,128)(2,1)S(1)}, bf16[1,512]{1,0:T(2,128)(2,1)}, u32[]{:S(2)}) %copy-start.4) | copy-done | bytes 1048
  0.7 0.0 copy-done.5
  0.7 0.0 copy-done.6
  0.7 0.0 copy-start
  0.7 1.0 %copy-done = f32[2,64,8,128]{3,2,1,0:T(8,128)S(1)} copy-done((f32[2,64,8,128]{3,2,1,0:T(8,128)S(1)}, f32[2,64,8,128]{3,2,1,0:T(8,128)}, u32[]{:S(2)}) %copy-start) | copy-done | bytes 524312
  1.7 0.0 copy-start.1
  1.7 1.0 %copy-done.1 = f32[2,64,8,128]{3,2,1,0:T(8,128)S(1)} copy-done((f32[2,64,8,128]{3,2,1,0:T(8,128)S(1)}, f32[2,64,8,128]{3,2,1,0:T(8,128)}, u32[]{:S(2)}) %copy-start.1) | copy-done | bytes 524312
  2.8 0.0 copy-start.2
  2.8 0.9 %copy-done.2 = bf16[1,256,512]{2,1,0:T(8,128)(2,1)S(1)} copy-done((bf16[1,256,512]{2,1,0:T(8,128)(2,1)S(1)}, bf16[1,256,512]{2,1,0:T(8,128)(2,1)}, u32[]{:S(2)}) %copy-start.2) | copy-done | bytes 262168
  3.7 0.0 copy-start.3
  3.7 0.9 %copy-done.3 = bf16[1,512,256]{2,1,0:T(8,128)(2,1)S(1)} copy-done((bf16[1,512,256]{2,1,0:T(8,128)(2,1)S(1)}, bf16[1,512,256]{2,1,0:T(8,128)(2,1)}, u32[]{:S(2)}) %copy-start.3) | copy-done | bytes 262168
  4.7 43.2 %shard_map.73 = f32[1024,128]{1,0:T(8,128)S(1)} custom-call(f32[1024,128]{1,0:T(8,128)S(1)} %bitcast.5, f32[1024,128]{1,0:T(8,128)S(1)} %bitcast.6, s32[1,8]{1,0:T(1,128)S(1)} %bitcast.7, bf16[1,256,512]{2,1,0:T(8,128)(2,1)S(1)} %copy-done.2, bf16[1,512]{1,0:T(2,128)(2,1)S(1)} %copy-done.4, bf16[1,512,256]{2,1,0:T(8,128)(2,1)S(1)} %copy-done.3, ...), custom_call_target="tpu_custom_call" | custom-call | tf_op jit(solution)/shard_map/pallas_call | solution.py:325
  47.9 0.8 %copy.9 = f32[2,64,8,128]{3,2,1,0:T(8,128)} copy(f32[2,64,8,128]{3,2,1,0:T(8,128)S(1)} %bitcast.4) | data formatting | bytes 1048576
Async XLA Ops:
  0.0 0.7 %copy-start.4 = (bf16[1,512]{1,0:T(2,128)(2,1)S(1)}, bf16[1,512]{1,0:T(2,128)(2,1)}, u32[]{:S(2)}) copy-start(bf16[1,512]{1,0:T(2,128)(2,1)} %bi_ref.1) | copy-start | bytes 3076
  0.0 0.7 %copy-start.5 = (s32[1,8,1]{1,2,0:T(1,128)S(1)}, s32[1,8,1]{1,2,0:T(1,128)}, u32[]{:S(2)}) copy-start(s32[1,8,1]{1,2,0:T(1,128)} %param.9) | copy-start | bytes 100
  0.0 0.7 %copy-start.6 = (bf16[1,128]{1,0:T(2,128)(2,1)S(1)}, bf16[1,128]{1,0:T(2,128)(2,1)}, u32[]{:S(2)}) copy-start(bf16[1,128]{1,0:T(2,128)(2,1)} %bo_ref.1) | copy-start | bytes 772
  0.7 1.0 %copy-start = (f32[2,64,8,128]{3,2,1,0:T(8,128)S(1)}, f32[2,64,8,128]{3,2,1,0:T(8,128)}, u32[]{:S(2)}) copy-start(f32[2,64,8,128]{3,2,1,0:T(8,128)} %param.7) | copy-start | bytes 1572868
  1.7 1.0 %copy-start.1 = (f32[2,64,8,128]{3,2,1,0:T(8,128)S(1)}, f32[2,64,8,128]{3,2,1,0:T(8,128)}, u32[]{:S(2)}) copy-start(f32[2,64,8,128]{3,2,1,0:T(8,128)} %param.8) | copy-start | bytes 1572868
  2.8 0.9 %copy-start.2 = (bf16[1,256,512]{2,1,0:T(8,128)(2,1)S(1)}, bf16[1,256,512]{2,1,0:T(8,128)(2,1)}, u32[]{:S(2)}) copy-start(bf16[1,256,512]{2,1,0:T(8,128)(2,1)} %wi_ref.1) | copy-start | bytes 786436
  3.7 0.9 %copy-start.3 = (bf16[1,512,256]{2,1,0:T(8,128)(2,1)S(1)}, bf16[1,512,256]{2,1,0:T(8,128)(2,1)}, u32[]{:S(2)}) copy-start(bf16[1,512,256]{2,1,0:T(8,128)(2,1)} %wo_ref.1) | copy-start | bytes 786436

commit v2 on v1

--- a/solution.py
+++ b/solution.py
@@ -34,9 +34,9 @@
 
 def kernel(
     sizes,
-    tr_ref, wd_ref, sc_ref, wi_ref, bi_ref, wo_ref, bo_ref,
+    tr_hbm, wd_hbm, sc_ref, wi_ref, bi_ref, wo_ref, bo_ref,
     out_ref,
-    hs, hr, pack, rp, tt, q1, h1, st, xbuf, pbuf, rbuf, wi_all, wo_all, bias,
+    tr_ref, wd_ref, hs, hr, pack, rp, tt, q1, h1, st, xbuf, pbuf, rbuf, wi_all, wo_all, bias,
     hs_sem, hr_sem, ps_sem, pr_sem, loc_sem, a_send, a_recv, b_send, b_recv,
     xs_sem, xr_sem, ys_sem, yr_sem,
 ):
@@ -55,6 +55,15 @@
     def peer_of(k):
         other = lax.rem(p + k, nband * 2)
         return {"band": other // 2, "lat": pair + lax.rem(other, 2)}, other
+
+    local = [
+        pltpu.make_async_copy(tr_hbm, tr_ref, loc_sem.at[2]),
+        pltpu.make_async_copy(wd_hbm, wd_ref, loc_sem.at[3]),
+        pltpu.make_async_copy(wi_ref.at[0], wi_all.at[z], loc_sem.at[0]),
+        pltpu.make_async_copy(wo_ref.at[0], wo_all.at[z], loc_sem.at[1]),
+    ]
+    for copy in local:
+        copy.start()
 
     barrier = pltpu.get_barrier_semaphore()
     for d in range(1, nlon):
@@ -73,6 +82,8 @@
     def own(ref, j):
         return ref[pl.ds(j, 128, stride=clon), :]
 
+    local[0].wait()
+    local[1].wait()
     for slot, j in enumerate((0, 1, clon - 2, clon - 1)):
         hs[slot, 0] = own(tr_ref, j).astype(BF16)
         hs[slot, 1] = own(wd_ref, j).astype(BF16)
@@ -96,36 +107,10 @@
         ))
         halos[-1].start()
 
-    lane = lax.broadcasted_iota(jnp.int32, (128, 128), 1)
-    acc = jnp.zeros((128, 128), F32)
-    for base, ref in ((0, tr_ref), (32, wd_ref)):
-        for j in range(clon):
-            x = own(ref, j)
-            for g, col in enumerate((0, 1, 126, 127)):
-                place = base + g * 8 + j
-                acc = jnp.where(lane == place, pltpu.roll(x, (place - col) % 128, 1), acc)
-    pack[...] = acc.astype(BF16)
-
-    def pack_copy(side, d):
-        return pltpu.make_async_remote_copy(
-            src_ref=pack, dst_ref=rp.at[side, 1 - d],
-            send_sem=ps_sem.at[side, 1 - d], recv_sem=pr_sem.at[side, 1 - d],
-            device_id={"lat": a + (1 if side == 0 else -1), "lon": lon_at(d)}, device_id_type=MESH,
-        )
-
-    for has, side in ((has_low, 1), (has_high, 0)):
-        @pl.when(has)
-        def _(side=side):
-            for d in (0, 1, -1):
-                pack_copy(side, d).start()
-
-    local = [
-        pltpu.make_async_copy(wi_ref.at[0], wi_all.at[z], loc_sem.at[0]),
-        pltpu.make_async_copy(wo_ref.at[0], wo_all.at[z], loc_sem.at[1]),
-    ]
     cut_i, cut_o = pl.ds(p * rows_i, rows_i), pl.ds(p * rows_o, rows_o)
+    order = sorted(range(1, nlon), key=lambda d: min(d, nlon - d))
     firsts = []
-    for d in range(1, nlon):
+    for d in order:
         trio = []
         for kind, (src, dst) in enumerate((
             (wi_ref.at[0, cut_i], wi_all.at[z, cut_i]),
@@ -138,14 +123,35 @@
                 device_id={"lon": lon_at(d)}, device_id_type=MESH,
             ))
             trio[-1].start()
-        firsts.append(trio)
-    for copy in local:
-        copy.start()
+        firsts.append((d, trio))
+
+    lane = lax.broadcasted_iota(jnp.int32, (128, 128), 1)
+    acc = jnp.zeros((128, 128), F32)
+    for base, ref in ((0, tr_ref), (32, wd_ref)):
+        for j in range(clon):
+            x = own(ref, j)
+            for g, col in enumerate((0, 1, 126, 127)):
+                place = base + g * 8 + j
+                acc = jnp.where(lane == place, pltpu.roll(x, (place - col) % 128, 1), acc)
+    pack[...] = acc.astype(BF16)
+
+    def pack_copy(side, d):
+        return pltpu.make_async_remote_copy(
+            src_ref=pack, dst_ref=rp.at[side, 1 - d],
+            send_sem=ps_sem.at[side, 1 - d], recv_sem=pr_sem.at[side, 1 - d],
+            device_id={"lat": a + (1 if side == 0 else -1), "lon": lon_at(d)}, device_id_type=MESH,
+        )
+
+    for has, side in ((has_low, 1), (has_high, 0)):
+        @pl.when(has)
+        def _(side=side):
+            for d in (0, 1, -1):
+                pack_copy(side, d).start()
 
     seconds = []
 
-    def forward(d):
-        for copy in firsts[d - 1]:
+    def forward(d, trio):
+        for copy in trio:
             copy.wait_recv()
         c = lon_at(-d)
         for k in range(1, nband * 2):
@@ -157,6 +163,49 @@
                 )
                 copy.start()
                 seconds.append(copy)
+
+    def shifted(x, rim, low_lane, high_lane):
+        ln = lane[: x.shape[0]]
+        south = jnp.where(ln == 0, pltpu.roll(rim, (128 - low_lane) % 128, 1), pltpu.roll(x, 1, 1))
+        north = jnp.where(
+            ln == 127, pltpu.roll(rim, (127 - high_lane) % 128, 1), pltpu.roll(x, 127, 1)
+        )
+        return south, north
+
+    def field(r):
+        if r < 0:
+            return hr[0, 2 + r, 0].astype(F32)
+        if r >= clon:
+            return hr[1, r - clon, 0].astype(F32)
+        return own(tr_ref, r)
+
+    def zonal(r):
+        if r < 0:
+            return hr[0, 2 + r, 1, :64].astype(F32)
+        if r >= clon:
+            return hr[1, r - clon, 1, :64].astype(F32)
+        return wd_ref[pl.ds(r, 64, stride=clon), :]
+
+    def merid(r):
+        if r < 0:
+            return hr[0, 2 + r, 1, 64:].astype(F32)
+        if r >= clon:
+            return hr[1, r - clon, 1, 64:].astype(F32)
+        return wd_ref[pl.ds(64 * clon + r, 64, stride=clon), :]
+
+    def rim_of(r):
+        return (0, clon - 1) if r < 0 else (2, 0) if r >= clon else (1, r)
+
+    def advance(r, get, rim):
+        slot, j = rim_of(r)
+        v = merid(r)
+        v_s, v_n = shifted(v, tt[slot, 64:, :], 56 + j, 32 + j)
+        q = get(r)
+        south, north = shifted(q, rim, 24 + j, j)
+        return step(
+            q, get(r - 1), get(r + 1), south, north,
+            zonal(r - 1), zonal(r), zonal(r + 1), v_s, v, v_n,
+        )
 
     for has, side in ((has_low, 0), (has_high, 1)):
         @pl.when(has)
@@ -193,52 +242,12 @@
     outside = jnp.where(lane >= 16, a, nlat - 1 - a) > 0
     h1[...] = jnp.where(outside, outer, 0.0)
 
-    def shifted(x, rim, low_lane, high_lane):
-        ln = lane[: x.shape[0]]
-        south = jnp.where(ln == 0, pltpu.roll(rim, (128 - low_lane) % 128, 1), pltpu.roll(x, 1, 1))
-        north = jnp.where(
-            ln == 127, pltpu.roll(rim, (127 - high_lane) % 128, 1), pltpu.roll(x, 127, 1)
-        )
-        return south, north
-
-    def field(r):
-        if r < 0:
-            return hr[0, 2 + r, 0].astype(F32)
-        if r >= clon:
-            return hr[1, r - clon, 0].astype(F32)
-        return own(tr_ref, r)
-
-    def zonal(r):
-        if r < 0:
-            return hr[0, 2 + r, 1, :64].astype(F32)
-        if r >= clon:
-            return hr[1, r - clon, 1, :64].astype(F32)
-        return wd_ref[pl.ds(r, 64, stride=clon), :]
-
-    def merid(r):
-        if r < 0:
-            return hr[0, 2 + r, 1, 64:].astype(F32)
-        if r >= clon:
-            return hr[1, r - clon, 1, 64:].astype(F32)
-        return wd_ref[pl.ds(64 * clon + r, 64, stride=clon), :]
-
-    def rim_of(r):
-        return (0, clon - 1) if r < 0 else (2, 0) if r >= clon else (1, r)
-
-    def advance(r, get, rim):
-        slot, j = rim_of(r)
-        v = merid(r)
-        v_s, v_n = shifted(v, tt[slot, 64:, :], 56 + j, 32 + j)
-        q = get(r)
-        south, north = shifted(q, rim, 24 + j, j)
-        return step(
-            q, get(r - 1), get(r + 1), south, north,
-            zonal(r - 1), zonal(r), zonal(r + 1), v_s, v, v_n,
-        )
-
+    forward(*firsts[0])
     inner = list(range(1, clon - 1))
     for r in inner:
         q1[r + 1] = advance(r, field, tt[1])
+    for item in firsts[1:2]:
+        forward(*item)
     for copy in halos:
         copy.wait_recv()
     for r in (-1, 0, clon - 1, clon):
@@ -256,42 +265,48 @@
         st[r] = new
         xbuf[l, r] = new.T.astype(BF16)
         x_copy(r).start()
-
-    for d in range(1, nlon):
-        forward(d)
+        if r == 1:
+            for item in firsts[2:]:
+                forward(*item)
+
     for copy in seconds:
         copy.wait_recv()
-    for copy in local:
-        copy.wait()
-
-    def y_copy(j):
+    local[2].wait()
+    local[3].wait()
+
+    half = clon // 2
+
+    def y_copy(g):
         return pltpu.make_async_remote_copy(
-            src_ref=pbuf.at[j, 1 - l], dst_ref=rbuf.at[j],
-            send_sem=ys_sem.at[j], recv_sem=yr_sem.at[j],
+            src_ref=pbuf.at[1 - l, pl.ds(g * half, half)], dst_ref=rbuf.at[pl.ds(g * half, half)],
+            send_sem=ys_sem.at[g], recv_sem=yr_sem.at[g],
             device_id={"lev": 1 - l}, device_id_type=MESH,
         )
 
     hid = bi_ref.shape[1]
-
-    @pl.loop(0, clon)
-    def _(j):
+    for j in range(clon):
         x_copy(j).wait_recv()
-        c = sc_ref[0, j]
-        x = jnp.concatenate([xbuf[0, j], xbuf[1, j]], axis=1)
-        pre = jnp.dot(x, wi_all[c], preferred_element_type=F32) + bias[c][0:1, :hid].astype(F32)
-        hidden = (pre * jax.nn.sigmoid(pre)).astype(BF16)
-        part = jnp.dot(hidden, wo_all[c], preferred_element_type=F32).astype(BF16)
-        pbuf[j, 0] = part[:, :128]
-        pbuf[j, 1] = part[:, 128:]
-        y_copy(j).start()
-
-    @pl.loop(0, clon)
-    def _(j):
-        y_copy(j).wait_recv()
-        c = sc_ref[0, j]
-        total = pbuf[j, l].astype(F32) + rbuf[j].astype(F32)
-        tend = (total + bias[c][0:1, hid:].astype(F32)).astype(BF16).astype(F32)
-        out_ref[pl.ds(j, 128, stride=clon), :] = st[j] + 0.5 * tend.T
+    classes = [sc_ref[0, j] for j in range(clon)]
+    for g in range(2):
+        group = range(g * half, (g + 1) * half)
+        hidden = []
+        for j in group:
+            x = jnp.concatenate([xbuf[0, j], xbuf[1, j]], axis=1)
+            pre = jnp.dot(x, wi_all[classes[j]], preferred_element_type=F32)
+            pre = pre + bias[classes[j]][0:1, :hid].astype(F32)
+            hidden.append((pre * jax.nn.sigmoid(pre)).astype(BF16))
+        for j, value in zip(group, hidden):
+            part = jnp.dot(value, wo_all[classes[j]], preferred_element_type=F32).astype(BF16)
+            pbuf[0, j] = part[:, :128]
+            pbuf[1, j] = part[:, 128:]
+        y_copy(g).start()
+
+    for g in range(2):
+        y_copy(g).wait_recv()
+        for j in range(g * half, (g + 1) * half):
+            total = pbuf[l, j].astype(F32) + rbuf[j].astype(F32)
+            tend = (total + bias[classes[j]][0:1, hid:].astype(F32)).astype(BF16).astype(F32)
+            out_ref[pl.ds(j, 128, stride=clon), :] = st[j] + 0.5 * tend.T
 
     for copy in halos:
         copy.wait_send()
@@ -300,7 +315,7 @@
         def _(side=side):
             for d in (0, 1, -1):
                 pack_copy(side, d).wait_send()
-    for trio in firsts:
+    for _, trio in firsts:
         for copy in trio:
             copy.wait_send()
     for copy in seconds:
@@ -309,7 +324,9 @@
     @pl.loop(0, clon)
     def _(j):
         x_copy(j).wait_send()
-        y_copy(j).wait_send()
+
+    for g in range(2):
+        y_copy(g).wait_send()
 
 
 def shards(sizes, tracers, winds, surface_class, w_in, b_in, w_out, b_out):
@@ -320,14 +337,16 @@
     members = nband * 2
     vmem = pl.BlockSpec(memory_space=pltpu.VMEM)
     smem = pl.BlockSpec(memory_space=pltpu.SMEM)
-    anywhere = pl.BlockSpec(memory_space=pl.ANY)
+    hbm = pl.BlockSpec(memory_space=pltpu.HBM)
     dma = pltpu.SemaphoreType.DMA
     new = pl.pallas_call(
         functools.partial(kernel, sizes),
         out_shape=jax.ShapeDtypeStruct(flat, F32),
-        in_specs=[vmem, vmem, smem, anywhere, vmem, anywhere, vmem],
+        in_specs=[hbm, hbm, smem, hbm, vmem, hbm, vmem],
         out_specs=vmem,
         scratch_shapes=[
+            pltpu.VMEM(flat, F32),
+            pltpu.VMEM(flat, F32),
             pltpu.VMEM((4, 2, rows, clat), BF16),
             pltpu.VMEM((2, 2, 2, rows, clat), BF16),
             pltpu.VMEM((rows, clat), BF16),
@@ -337,17 +356,17 @@
             pltpu.VMEM((rows, clat), F32),
             pltpu.VMEM((clon, rows, clat), F32),
             pltpu.VMEM((2, clon, clat, rows), BF16),
-            pltpu.VMEM((clon, 2, clat, rows), BF16),
+            pltpu.VMEM((2, clon, clat, rows), BF16),
             pltpu.VMEM((clon, clat, rows), BF16),
             pltpu.VMEM((nlon,) + w_in.shape[1:], BF16),
             pltpu.VMEM((nlon,) + w_out.shape[1:], BF16),
             pltpu.VMEM((nlon, 16, b_in.shape[1] + b_out.shape[1]), BF16),
-            dma((2,)), dma((2,)), dma((2, 3)), dma((2, 3)), dma((2,)),
+            dma((2,)), dma((2,)), dma((2, 3)), dma((2, 3)), dma((4,)),
             dma((3, nlon)), dma((3, nlon)), dma((2, nlon, members)), dma((2, nlon, members)),
-            dma((clon,)), dma((clon,)), dma((clon,)), dma((clon,)),
+            dma((clon,)), dma((clon,)), dma((2,)), dma((2,)),
         ],
         compiler_params=pltpu.CompilerParams(
-            collective_id=0, has_side_effects=True, vmem_limit_bytes=48 * 1024 * 1024
+            collective_id=0, has_side_effects=True, vmem_limit_bytes=63 * 1024 * 1024
         ),
     )(tracers.reshape(flat), winds.reshape(flat), surface_class.reshape(1, clon), w_in, b_in, w_out, b_out)
     return new.reshape(tracers.shape)

time: 49 us -> 51.6 us (1.053)
  the two profiles are of different devices: /device:TPU:0 before, /device:TPU:13 now
where the time goes in v2:
time: 51.6 us; the launch traced here: 51.4 us
  Pallas kernels  49.5 us (96%)
  local copies, waits for them, and re-layouts  1.87 us (4%)
    pallas_call x1, Pallas kernels, shards(): pl.pallas_call(functools.partial(kernel, sizes), out_shape=jax.ShapeDtype...  49.5 us
    unnamed x1, local copies, waits for them, and re-layouts  1.87 us

profile of v2, /device:TPU:13, one launch (start us, length us, event | category | flops | bytes accessed | tf_op | source)
XLA Modules:
  0.0 51.4 jit_solution(15478576464559242345)
XLA Ops:
  0.0 49.5 %shard_map.73 = f32[1024,128]{1,0:T(8,128)} custom-call(f32[1024,128]{1,0:T(8,128)} %bitcast.5, f32[1024,128]{1,0:T(8,128)} %bitcast.6, s32[1,8]{1,0:T(1,128)} %bitcast.7, bf16[1,256,512]{2,1,0:T(8,128)(2,1)} %wi_ref.1, bf16[1,512]{1,0:T(2,128)(2,1)} %bi_ref.1, bf16[1,512,256]{2,1,0:T(8,128)(2,1)} %wo_ref.1, bf16[1,128]{1,0:T(2,128)(2,1)} %bo_ref.1), custom_call_target="tpu_custom_call" | custom-call | tf_op jit(solution)/shard_map/pallas_call | solution.py:342
  49.5 1.9 %copy.9 = f32[2,64,8,128]{3,2,1,0:T(8,128)} copy(f32[2,64,8,128]{3,2,1,0:T(8,128)} %bitcast.4) | data formatting | bytes 1048576

commit v3 on v2

--- a/solution.py
+++ b/solution.py
@@ -107,6 +107,29 @@
         ))
         halos[-1].start()
 
+    lane = lax.broadcasted_iota(jnp.int32, (128, 128), 1)
+    acc = jnp.zeros((128, 128), F32)
+    for base, ref in ((0, tr_ref), (32, wd_ref)):
+        for j in range(clon):
+            x = own(ref, j)
+            for g, col in enumerate((0, 1, 126, 127)):
+                place = base + g * 8 + j
+                acc = jnp.where(lane == place, pltpu.roll(x, (place - col) % 128, 1), acc)
+    pack[...] = acc.astype(BF16)
+
+    def pack_copy(side, d):
+        return pltpu.make_async_remote_copy(
+            src_ref=pack, dst_ref=rp.at[side, 1 - d],
+            send_sem=ps_sem.at[side, 1 - d], recv_sem=pr_sem.at[side, 1 - d],
+            device_id={"lat": a + (1 if side == 0 else -1), "lon": lon_at(d)}, device_id_type=MESH,
+        )
+
+    for has, side in ((has_low, 1), (has_high, 0)):
+        @pl.when(has)
+        def _(side=side):
+            for d in (0, 1, -1):
+                pack_copy(side, d).start()
+
     cut_i, cut_o = pl.ds(p * rows_i, rows_i), pl.ds(p * rows_o, rows_o)
     order = sorted(range(1, nlon), key=lambda d: min(d, nlon - d))
     firsts = []
@@ -124,29 +147,6 @@
             ))
             trio[-1].start()
         firsts.append((d, trio))
-
-    lane = lax.broadcasted_iota(jnp.int32, (128, 128), 1)
-    acc = jnp.zeros((128, 128), F32)
-    for base, ref in ((0, tr_ref), (32, wd_ref)):
-        for j in range(clon):
-            x = own(ref, j)
-            for g, col in enumerate((0, 1, 126, 127)):
-                place = base + g * 8 + j
-                acc = jnp.where(lane == place, pltpu.roll(x, (place - col) % 128, 1), acc)
-    pack[...] = acc.astype(BF16)
-
-    def pack_copy(side, d):
-        return pltpu.make_async_remote_copy(
-            src_ref=pack, dst_ref=rp.at[side, 1 - d],
-            send_sem=ps_sem.at[side, 1 - d], recv_sem=pr_sem.at[side, 1 - d],
-            device_id={"lat": a + (1 if side == 0 else -1), "lon": lon_at(d)}, device_id_type=MESH,
-        )
-
-    for has, side in ((has_low, 1), (has_high, 0)):
-        @pl.when(has)
-        def _(side=side):
-            for d in (0, 1, -1):
-                pack_copy(side, d).start()
 
     seconds = []
 

time: 51.6 us -> 42.6 us (0.83)
  the two profiles are of different devices: /device:TPU:13 before, /device:TPU:0 now
where the time goes in v3:
time: 42.6 us; the launch traced here: 42.3 us
  Pallas kernels  40.4 us (95%)
  local copies, waits for them, and re-layouts  1.87 us (4%)
    pallas_call x1, Pallas kernels, shards(): pl.pallas_call(functools.partial(kernel, sizes), out_shape=jax.ShapeDtype...  40.4 us
    unnamed x1, local copies, waits for them, and re-layouts  1.87 us

profile of v3, /device:TPU:0, one launch (start us, length us, event | category | flops | bytes accessed | tf_op | source)
XLA Modules:
  0.0 42.3 jit_solution(9375828399520695217)
XLA Ops:
  0.0 40.4 %shard_map.73 = f32[1024,128]{1,0:T(8,128)} custom-call(f32[1024,128]{1,0:T(8,128)} %bitcast.5, f32[1024,128]{1,0:T(8,128)} %bitcast.6, s32[1,8]{1,0:T(1,128)} %bitcast.7, bf16[1,256,512]{2,1,0:T(8,128)(2,1)} %wi_ref.1, bf16[1,512]{1,0:T(2,128)(2,1)} %bi_ref.1, bf16[1,512,256]{2,1,0:T(8,128)(2,1)} %wo_ref.1, bf16[1,128]{1,0:T(2,128)(2,1)} %bo_ref.1), custom_call_target="tpu_custom_call" | custom-call | tf_op jit(solution)/shard_map/pallas_call | solution.py:342
  40.4 1.9 %copy.9 = f32[2,64,8,128]{3,2,1,0:T(8,128)} copy(f32[2,64,8,128]{3,2,1,0:T(8,128)} %bitcast.4) | data formatting | bytes 1048576

commit v4 on v3

--- a/solution.py
+++ b/solution.py
@@ -265,7 +265,7 @@
         st[r] = new
         xbuf[l, r] = new.T.astype(BF16)
         x_copy(r).start()
-        if r == 1:
+        if r == clon - 1:
             for item in firsts[2:]:
                 forward(*item)
 

time: 42.6 us -> 42.6 us (level)
  no operation moved by 1% of the time
where the time goes in v4:
time: 42.6 us; the launch traced here: 42.3 us
  Pallas kernels  40.4 us (95%)
  local copies, waits for them, and re-layouts  1.87 us (4%)
    pallas_call x1, Pallas kernels, shards(): pl.pallas_call(functools.partial(kernel, sizes), out_shape=jax.ShapeDtype...  40.4 us
    unnamed x1, local copies, waits for them, and re-layouts  1.87 us

profile of v4, /device:TPU:0, one launch (start us, length us, event | category | flops | bytes accessed | tf_op | source)
XLA Modules:
  0.0 42.3 jit_solution(3705981180428690340)
XLA Ops:
  0.0 40.4 %shard_map.73 = f32[1024,128]{1,0:T(8,128)} custom-call(f32[1024,128]{1,0:T(8,128)} %bitcast.5, f32[1024,128]{1,0:T(8,128)} %bitcast.6, s32[1,8]{1,0:T(1,128)} %bitcast.7, bf16[1,256,512]{2,1,0:T(8,128)(2,1)} %wi_ref.1, bf16[1,512]{1,0:T(2,128)(2,1)} %bi_ref.1, bf16[1,512,256]{2,1,0:T(8,128)(2,1)} %wo_ref.1, bf16[1,128]{1,0:T(2,128)(2,1)} %bo_ref.1), custom_call_target="tpu_custom_call" | custom-call | tf_op jit(solution)/shard_map/pallas_call | solution.py:342
  40.4 1.9 %copy.9 = f32[2,64,8,128]{3,2,1,0:T(8,128)} copy(f32[2,64,8,128]{3,2,1,0:T(8,128)} %bitcast.4) | data formatting | bytes 1048576
